TPU v7x, 32 devices: a whole 2x2x4 slice. The times are simulated.
32 devices in a mesh: row: 8 (over z, core), col: 4 (over y, x).
Axes of the slice: x: 2, y: 2, z: 4, core: 2. Of those that a mesh axis runs over, the one named last changes fastest.
Arguments:
- query: bfloat16 [192, 1024, 128], P('row', 'col'), may hold values from -12 to 12
- key: bfloat16 [192, 1024, 128], P('row', 'col'), may hold values from -6 to 6
- value: bfloat16 [192, 1024, 128], P('row', 'col'), may hold values from -6 to 6
- gate: bfloat16 [192, 1024, 128], P('row', 'col'), may hold values from -6 to 6
- d_out: bfloat16 [192, 1024, 128], P('row', 'col'), may hold values from -6 to 6
- bias: bfloat16 [4, 1024, 1024], P(None, 'col'), may hold values from -6 to 6
- length: int32 [1], replicated, may hold values from 513 to 1024
Outputs:
- d_query: bfloat16 [192, 1024, 128], P('row', 'col')
- d_key: bfloat16 [192, 1024, 128], P('row', 'col')
- d_value: bfloat16 [192, 1024, 128], P('row', 'col')
- d_gate: bfloat16 [192, 1024, 128], P('row', 'col')
- d_bias: float32 [4, 1024, 1024], P(None, 'row', 'col')
All inputs are finite; a program needn't handle non-finite values.
Results may differ from a plain program's by a relative error of at most 0.014.
Values may be sent and summed in bfloat16 or wider, within the bound.
No kernel may reach another device: no remote copies, remote signals or barrier semaphores. Data moves between devices by JAX's collectives and lax.ppermute only.
A program may use at most 128 MiB of HBM per device.

v0:
```python
import functools
import itertools

import jax
import jax.numpy as jnp
from jax import lax
from jax.experimental import pallas as pl
from jax.experimental.pallas import tpu as pltpu
from jax.sharding import PartitionSpec as P

LOG2E = 1.4426950408889634
MASKED = -1e30
SHARES = (1, 3, 4, 4)
PIECES = 4


def dot(a, b, dims):
    return lax.dot_general(a, b, (dims, ((), ())), preferred_element_type=jnp.float32)


def peer_of(me, step):
    return jnp.bitwise_xor(me, step)


def pack_kernel(heads, groups, with_bias, info, q_ref, k_ref, v_ref, g_ref, o_ref, *refs):
    n_col = heads * groups
    outs, turned = refs[-1 - n_col : -1], refs[-1]
    me = info[1]
    count, _, channels = q_ref.shape[1:]
    c = channels // heads
    lines = count * PIECES * c
    for i in range(count):
        for g in range(groups):
            gated = o_ref[g, i].astype(jnp.float32) * jax.nn.sigmoid(g_ref[g, i].astype(jnp.float32))
            pieces = (q_ref[g, i], k_ref[g, i], v_ref[g, i], gated.astype(jnp.bfloat16))
            for piece, x in enumerate(pieces):
                turned[g, i, piece] = x.T
        for step in range(n_col):
            peer = peer_of(me, step)
            head = pl.multiple_of(peer // groups * c, c)
            base = outs[step].shape[0] - lines
            for piece in range(PIECES):
                at = base + (i * PIECES + piece) * c
                outs[step][at : at + c, :] = turned[peer % groups, i, piece, pl.ds(head, c), :]
    if with_bias:
        for step in range(n_col):
            base = outs[step].shape[0] - lines
            keys = pl.ds(pl.multiple_of(info[2] * base, base), base) if step else slice(None)
            outs[step][:base, :] = refs[0][peer_of(me, step) // groups, :, keys].T


def unpack_kernel(heads, groups, info, g_ref, o_ref, *refs):
    n_col = heads * groups
    ins, (dq, dk, dv, dg, token, whole) = refs[:n_col], refs[-6:]
    token[...] = jnp.zeros_like(token)
    me = info[1]
    count, _, channels = g_ref.shape[1:]
    c = channels // heads
    for i in range(count):
        for step in range(n_col):
            peer = peer_of(me, step)
            head = pl.multiple_of(peer // groups * c, c)
            for piece in range(PIECES):
                at = (i * PIECES + piece) * c
                whole[peer % groups, i, piece, pl.ds(head, c), :] = ins[step][at : at + c, :]
        for g in range(groups):
            dq[g, i] = whole[g, i, 0].T
            dk[g, i] = whole[g, i, 1].T
            dv[g, i] = whole[g, i, 2].T
            attended = whole[g, i, 3].T.astype(jnp.float32)
            s = jax.nn.sigmoid(g_ref[g, i].astype(jnp.float32))
            dg[g, i] = (o_ref[g, i].astype(jnp.float32) * attended * s * (1.0 - s)).astype(jnp.bfloat16)


def woven(*queues):
    order = [(at / len(q), which, at) for which, q in enumerate(queues) for at in range(len(q))]
    for _, which, at in sorted(order):
        queues[which][at]()


def attention_kernel(n_col, together, c, scaling, first, last, info, *refs):
    bias_in, ins, refs = refs[: 2 * n_col - 1], refs[2 * n_col - 1 : 3 * n_col - 1], refs[3 * n_col - 1 :]
    scratch, refs = refs[-14:], refs[:-14]
    bias, total_s, q_s, g_s, k_s, v_s, k_turned, v_turned, dq_s, at_s, dkv, logits, weights, grads = scratch
    if not first:
        total_in = refs[0]
    totals = refs[-2:] if last else refs[-1:]
    outs, total_out = refs[-n_col - len(totals) : -len(totals)], totals[0]
    total = total_s if last else total_out
    length, me, side, level = info[0], info[1], info[2], info[3]
    blk = ins[0].shape[1]
    n = n_col * blk
    tile = min(256, n)
    tiles = range(0, n, tile)
    deep = k_s.shape[1]
    some = range(together)

    @pl.when(pl.program_id(0) == 0)
    def _():
        half = n // 2
        bias[me] = bias_in[0][...].astype(jnp.float32) * LOG2E
        for step in range(1, n_col):
            for table, which in ((bias_in[step], side), (bias_in[n_col + step - 1], 1 - side)):
                keys = pl.ds(pl.multiple_of(which * half, half), half)
                bias[peer_of(me, step), keys, :] = table[...].astype(jnp.float32) * LOG2E
        if first:
            total[...] = jnp.zeros_like(total)
        else:
            total[...] = total_in[...]
        rows = lax.broadcasted_iota(jnp.int32, (deep - 2 * c, n), 0)
        keys = lax.broadcasted_iota(jnp.int32, (deep - 2 * c, n), 1)
        mask = jnp.logical_and(rows == 0, keys >= length)
        for r in some:
            k_s[r, 2 * c :, :] = jnp.where(mask, MASKED, 0.0).astype(jnp.bfloat16)
            v_s[r, c:, :] = jnp.ones((deep - c, n), jnp.bfloat16)
            q_s[r, :, 2 * c :, :] = jnp.ones((n_col, deep - 2 * c, blk), jnp.bfloat16)

    def rows_of(r, piece):
        at = (r * PIECES + piece) * c
        return slice(at, at + c)

    for r in some:
        for step in range(n_col):
            jb = peer_of(me, step)
            span = pl.ds(pl.multiple_of(jb * blk, blk), blk)
            q = ins[step][rows_of(r, 0), :].astype(jnp.float32) * (scaling * LOG2E)
            high = q.astype(jnp.bfloat16)
            q_s[r, jb, :c, :] = high
            q_s[r, jb, c : 2 * c, :] = (q - high.astype(jnp.float32)).astype(jnp.bfloat16)
            k = ins[step][rows_of(r, 1), :]
            k_s[r, :c, span] = k
            k_s[r, c : 2 * c, span] = k
            v_s[r, :c, span] = ins[step][rows_of(r, 2), :]
            g_s[r, jb] = ins[step][rows_of(r, 3), :]
    for r in some:
        k_turned[r] = k_s[r].T
        v_turned[r] = v_s[r].T
    tops, scaled, scales = {}, {}, {}

    def score(jb, r, t):
        part = dot(k_turned[r, t : t + tile, :], q_s[r, jb], ((1,), (0,))) + bias[jb, t : t + tile, :]
        logits[jb % 2, r, t : t + tile, :] = part
        top = jnp.max(part.reshape(tile // 8, 8, blk), axis=0)
        tops[jb, r] = jnp.maximum(tops[jb, r], top) if t else top

    def expand(jb, r, t):
        if t == 0:
            tops[jb, r] = jnp.max(tops[jb, r], axis=0, keepdims=True)
        part = jnp.exp2(logits[jb % 2, r, t : t + tile, :] - tops[jb, r])
        weights[jb % 2, r, t : t + tile, :] = part.astype(jnp.bfloat16)

    def attend(jb, r):
        summed = dot(v_s[r, : c + 16, :], weights[jb % 2, r], ((1,), (0,)))
        inverse = 1.0 / summed[c : c + 1, :]
        attended = summed[:c, :] * inverse
        at_s[r, jb] = attended.astype(jnp.bfloat16)
        g = g_s[r, jb].astype(jnp.float32)
        row_dot = jnp.sum(g * attended, axis=0, keepdims=True) * (-inverse)
        high = row_dot.astype(jnp.bfloat16).astype(jnp.float32)
        rows = lax.broadcasted_iota(jnp.int32, (deep - c, blk), 0)
        tail = jnp.where(rows == 0, high, jnp.where(rows == 1, row_dot - high, 0.0))
        scaled[jb, r] = (g * inverse).astype(jnp.bfloat16)
        scales[jb, r] = jnp.concatenate([scaled[jb, r], tail.astype(jnp.bfloat16)], axis=0)

    def back(jb, t):
        added = total[jb, t : t + tile, :]
        for r in some:
            grad = dot(v_turned[r, t : t + tile, :], scales[jb, r], ((1,), (0,)))
            grad = grad * weights[jb % 2, r, t : t + tile, :].astype(jnp.float32)
            added = added + grad
            grads[jb % 2, r, t : t + tile, :] = grad.astype(jnp.bfloat16)
        total[jb, t : t + tile, :] = added

    def query_grad(jb, r):
        dq_s[r, jb] = (dot(k_s[r, :c, :], grads[jb % 2, r], ((1,), (0,))) * scaling).astype(jnp.bfloat16)

    def add_to(at, r, jb, part):
        if jb:
            part = part + dkv[r, at : at + c, :]
        dkv[r, at : at + c, :] = part

    def key_grad(jb, r):
        add_to(0, r, jb, dot(q_s[r, jb, :c, :], grads[jb % 2, r], ((1,), (1,))))

    def value_grad(jb, r):
        add_to(c, r, jb, dot(scaled[jb, r], weights[jb % 2, r], ((1,), (1,))))

    def each(step, jb, *ranges):
        if not 0 <= jb < n_col:
            return []
        return [functools.partial(step, jb, *at) for at in itertools.product(*ranges)]

    def finish(jb):
        return each(value_grad, jb, some) + each(query_grad, jb, some) + each(key_grad, jb, some)

    woven(each(score, 0, some, tiles))
    for jb in range(n_col):
        woven(each(expand, jb, some, tiles), finish(jb - 1))
        woven(each(attend, jb, some), each(score, jb + 1, some, tiles[: len(tiles) // 2]))
        woven(each(back, jb, tiles), each(score, jb + 1, some, tiles[len(tiles) // 2 :]))
    woven(finish(n_col - 1))

    for r in some:
        for step in range(n_col):
            jb = peer_of(me, step)
            span = pl.ds(pl.multiple_of(jb * blk, blk), blk)
            outs[step][rows_of(r, 0), :] = dq_s[r, jb]
            outs[step][rows_of(r, 1), :] = (dkv[r, :c, span] * (1.0 / LOG2E)).astype(jnp.bfloat16)
            outs[step][rows_of(r, 2), :] = dkv[r, c:, span].astype(jnp.bfloat16)
            outs[step][rows_of(r, 3), :] = at_s[r, jb]

    if last:

        @pl.when(pl.program_id(0) == pl.num_programs(0) - 1)
        def _():
            mine, others = totals
            pairs, _, width = mine.shape
            for pair in range(pairs):
                at = 2 * pair * width
                both = total[at // blk, :, at % blk : at % blk + 2 * width].astype(jnp.bfloat16)
                even, odd = both[:, :width], both[:, width:]
                mine[peer_of(level, pair)] = jnp.where(side == 0, even, odd)
                others[peer_of(level, pair)] = jnp.where(side == 0, odd, even)


def hold_kernel(*refs):
    pass


def params(mib):
    return pltpu.CompilerParams(
        dimension_semantics=("arbitrary",), vmem_limit_bytes=mib * 1024 * 1024
    )


def on_device(n_row, n_col, query, key, value, gate, d_out, bias, length):
    rows, blk, channels = query.shape
    heads, _, n = bias.shape
    c = channels // heads
    groups = n_col // heads
    share = rows // groups
    sizes = [share * weight // sum(SHARES) for weight in SHARES]
    starts = [sum(sizes[:m]) for m in range(len(sizes))]
    assert groups * heads == n_col and n == n_col * blk and groups * sum(sizes) == rows
    scaling = c ** (-0.5)
    per = 2 if all(size % 2 == 0 for size in sizes) else 1
    split_rows = (groups, share, blk, channels)
    query, key, value, gate, d_out = (x.reshape(split_rows) for x in (query, key, value, gate, d_out))
    row = lax.axis_index("row")
    info = jnp.stack([length[0], lax.axis_index("col"), row % 2, row // 2]).astype(jnp.int32)
    width = n // n_row
    lines = PIECES * c
    chunks = len(sizes)
    turned_shape = (groups, per, PIECES, channels, blk)

    untouched = pl.BlockSpec(memory_space=pl.ANY)

    def exchange(blocks):
        pairs = [[(a, a ^ step) for a in range(n_col)] for step in range(n_col)]
        return [blocks[0]] + [lax.ppermute(blocks[step], "col", pairs[step]) for step in range(1, n_col)]

    def swap(x):
        return lax.ppermute(x, "row", [(r, r ^ 1) for r in range(n_row)])

    def hold(blocks, until):
        count = len(blocks)
        return pl.pallas_call(
            hold_kernel,
            in_specs=[untouched] * (count + len(until)),
            out_specs=[untouched] * count,
            out_shape=[jax.ShapeDtypeStruct(x.shape, x.dtype) for x in blocks],
            input_output_aliases={a: a for a in range(count)},
            name="hold",
        )(*blocks, *until)

    def call(kernel, name, m, flops, grid, operands, out_specs, out_shape, scratch, aliases):
        return pl.pallas_call(
            kernel,
            grid_spec=pltpu.PrefetchScalarGridSpec(
                num_scalar_prefetch=1,
                grid=(grid,),
                in_specs=[spec for spec, _ in operands],
                out_specs=out_specs,
                scratch_shapes=scratch,
            ),
            out_shape=out_shape,
            input_output_aliases=aliases,
            compiler_params=params(60),
            cost_estimate=pl.CostEstimate(
                flops=sizes[m] * flops, bytes_accessed=sizes[m] * blk * channels * 18, transcendentals=0
            ),
            name=name,
        )(info, *[x for _, x in operands])

    def still(*shape):
        return pl.BlockSpec(shape, lambda i, info: (0,) * len(shape), pipeline_mode=pl.Buffered(1))

    def part(size, skip):
        return pl.BlockSpec((size, blk), lambda i, info: (skip + i, 0))

    def pack(m):
        with_bias = m == 0
        step = sizes[m] if with_bias else per
        base = starts[m] // step
        whole = pl.BlockSpec((groups, step, blk, channels), lambda i, info: (0, base + i, 0, 0))
        ahead = [n] + [n // 2] * (n_col - 1) if with_bias else [0] * n_col
        size = (sizes[m] + (sizes[m - 2] if m >= 2 else 0)) * lines
        operands = [(whole, x) for x in (query, key, value, gate, d_out)]
        if with_bias:
            operands.append((still(heads, blk, n), bias))
        return call(
            functools.partial(pack_kernel, heads, groups, with_bias),
            "pack",
            m,
            10**6,
            sizes[m] // step,
            operands,
            [part(x + step * lines, 0) for x in ahead],
            [jax.ShapeDtypeStruct((x + size, blk), jnp.bfloat16) for x in ahead],
            [pltpu.VMEM((groups, step, PIECES, channels, blk), jnp.bfloat16)],
            {},
        )

    def attend(m, total, bias_blocks, blocks, room):
        first, last = m == 0, m == chunks - 1

        def scratch(*shape, dtype=jnp.bfloat16):
            return pltpu.VMEM((per, *shape), dtype)

        operands = [(still(n if a == 0 else n // 2, blk), x) for a, x in enumerate(bias_blocks)]
        for a, x in enumerate(blocks):
            skip = (n if a == 0 else n // 2) // (per * lines) if first else 0
            operands.append((part(per * lines, skip), x))
        square = (n_col, n, blk)
        if not first:
            operands.append((still(*square), total))
        aliases, ahead = {}, 0
        if room is not None:
            aliases = {1 + len(operands) + a: a for a in range(n_col)}
            operands += [(untouched, x) for x in room]
            ahead = sizes[m + 2] // per
            out_shape = [jax.ShapeDtypeStruct(x.shape, x.dtype) for x in room]
        else:
            out_shape = [jax.ShapeDtypeStruct((sizes[m] * lines, blk), jnp.bfloat16)] * n_col
        if last:
            totals = [jax.ShapeDtypeStruct((n_row // 2, n, width), jnp.bfloat16)] * 2
        else:
            totals = [jax.ShapeDtypeStruct(square, jnp.float32)]
        deep = 4 * c
        result = call(
            functools.partial(attention_kernel, n_col, per, c, scaling, first, last),
            "attend",
            m,
            4 * 10**9,
            sizes[m] // per,
            operands,
            [part(per * lines, ahead)] * n_col + [still(*x.shape) for x in totals],
            out_shape + totals,
            [
                pltpu.VMEM(square, jnp.float32),
                pltpu.VMEM(square if last else (8, 128), jnp.float32),
                scratch(n_col, deep, blk),
                scratch(n_col, c, blk),
                scratch(deep, n),
                scratch(deep, n),
                scratch(n, deep),
                scratch(n, deep),
                scratch(n_col, c, blk),
                scratch(n_col, c, blk),
                scratch(2 * c, n, dtype=jnp.float32),
                pltpu.VMEM((2, per, n, blk), jnp.float32),
                pltpu.VMEM((2, per, n, blk), jnp.bfloat16),
                pltpu.VMEM((2, per, n, blk), jnp.bfloat16),
            ],
            aliases,
        )
        return result[:n_col], result[n_col:]

    def unpack(m, blocks, grads):
        base = starts[m] // per
        ahead = sizes[m + 2] // per if m + 2 < chunks else 0
        whole = pl.BlockSpec((groups, per, blk, channels), lambda i, info: (0, base + i, 0, 0))
        kept = [] if grads is None else list(grads)
        operands = [(whole, gate), (whole, d_out)]
        operands += [(part(per * lines, ahead), x) for x in blocks]
        aliases = {1 + len(operands) + a: a for a in range(len(kept))}
        operands += [(untouched, x) for x in kept]
        return call(
            functools.partial(unpack_kernel, heads, groups),
            "unpack",
            m,
            10**6,
            sizes[m] // per,
            operands,
            [whole] * 4 + [pl.BlockSpec((8, 128), lambda i, info: (0, 0))],
            [jax.ShapeDtypeStruct(query.shape, jnp.bfloat16)] * 4
            + [jax.ShapeDtypeStruct((8, 128), jnp.float32)],
            [pltpu.VMEM(turned_shape, jnp.bfloat16)],
            aliases,
        )

    packed = [pack(m) for m in range(chunks)]
    own, *fetched = exchange(packed[0])
    fetched = hold(fetched, [x[0] for x in packed[1:]])
    tables = [own, *fetched] + [swap(x[: n // 2]) for x in fetched]
    later = hold(packed[1][1:], fetched)
    arrived = [[own, *fetched], exchange([packed[1][0], *later])]
    totals, grads = [None], None
    for m in range(chunks):
        room = packed[m + 2] if m + 2 < chunks else None
        results, totals = attend(m, totals[0], tables, arrived[m], room)
        arrived.append(exchange(results))
    for m in range(chunks):
        *grads, token = unpack(m, arrived[m + 2], grads)

    mine, others = totals
    (others,) = hold([others], arrived[chunks][1:])
    others = swap(others)
    shares = []
    for step in range(n_row // 2):
        share = mine[step].astype(jnp.float32) + others[step].astype(jnp.float32)
        pairs = [(r, r ^ (2 * step)) for r in range(n_row)]
        share = share.astype(jnp.bfloat16)
        shares.append(lax.ppermute(share, "row", pairs) if step else share)
    total = sum(x.astype(jnp.float32) for x in shares) + token[0, 0]
    total = total.astype(jnp.bfloat16).reshape(n_col, blk, width)
    total = lax.all_to_all(total, "col", split_axis=0, concat_axis=0, tiled=True)
    total = jnp.sum(total.reshape(heads, groups, blk, width).astype(jnp.float32), axis=1)
    bias_grad = jnp.transpose(total, (0, 2, 1))
    d_query, d_key, d_value, d_gate = (x.reshape(rows, blk, channels) for x in grads)
    return d_query, d_key, d_value, d_gate, bias_grad


def solution(mesh):
    pair = P("row", "col", None)
    return jax.shard_map(
        functools.partial(on_device, mesh.shape["row"], mesh.shape["col"]),
        mesh=mesh,
        in_specs=(pair, pair, pair, pair, pair, P(None, "col", None), P()),
        out_specs=(pair, pair, pair, pair, P(None, "row", "col")),
        check_vma=False,
    )
```

profile of v0, /device:TPU:18, one launch (start us, length us, event | category | flops | bytes accessed | tf_op | source)
XLA Modules:
  0.0 207.0 jit_solution(6020854932359471894)
XLA Ops:
  1.9 4.1 %pack.4 = (bf16[1280,256]{1,0:T(8,128)(2,1)}, bf16[768,256]{1,0:T(8,128)(2,1)}, bf16[768,256]{1,0:T(8,128)(2,1)}, bf16[768,256]{1,0:T(8,128)(2,1)}) custom-call(s32[4]{0:T(128)} %pad_add_fusion.info, bf16[1,24,256,128]{3,2,1,0:T(8,128)(2,1)} %bitcast.43, bf16[1,24,256,128]{3,2,1,0:T(8,128)(2,1)} %bitcast.47, bf16[1,24,256,128]{3,2,1,0:T(8,128)(2,1)} %bitcast.51, ...), custom_call_target="tpu_custom_call" | custom-call | flops 2000000 | bytes 1179648 | tf_op jit(solution)/shard_map/pack/pallas_call | solution.py:277
  6.5 1.5 collective-permute-start.1
  8.0 1.4 collective-permute-start.2
  9.5 4.6 %pack.5 = (bf16[768,256]{1,0:T(8,128)(2,1)}, bf16[768,256]{1,0:T(8,128)(2,1)}, bf16[768,256]{1,0:T(8,128)(2,1)}, bf16[768,256]{1,0:T(8,128)(2,1)}) custom-call(s32[4]{0:T(128)} %pad_add_fusion.info, bf16[1,24,256,128]{3,2,1,0:T(8,128)(2,1)} %bitcast.44, bf16[1,24,256,128]{3,2,1,0:T(8,128)(2,1)} %bitcast.48, bf16[1,24,256,128]{3,2,1,0:T(8,128)(2,1)} %bitcast.52, ...), custom_call_target="tpu_custom_call" | custom-call | flops 6000000 | bytes 3538944 | tf_op jit(solution)/shard_map/pack/pallas_call | solution.py:277
  14.1 5.0 %pack.6 = (bf16[1280,256]{1,0:T(8,128)(2,1)}, bf16[1280,256]{1,0:T(8,128)(2,1)}, bf16[1280,256]{1,0:T(8,128)(2,1)}, bf16[1280,256]{1,0:T(8,128)(2,1)}) custom-call(s32[4]{0:T(128)} %pad_add_fusion.info, bf16[1,24,256,128]{3,2,1,0:T(8,128)(2,1)} %bitcast.45, bf16[1,24,256,128]{3,2,1,0:T(8,128)(2,1)} %bitcast.49, bf16[1,24,256,128]{3,2,1,0:T(8,128)(2,1)} %bitcast.53, ...), custom_call_target="tpu_custom_call" | custom-call | flops 8000000 | bytes 4718592 | tf_op jit(solution)/shard_map/pack/pallas_call | solution.py:277
  19.1 4.9 %pack.7 = (bf16[1792,256]{1,0:T(8,128)(2,1)}, bf16[1792,256]{1,0:T(8,128)(2,1)}, bf16[1792,256]{1,0:T(8,128)(2,1)}, bf16[1792,256]{1,0:T(8,128)(2,1)}) custom-call(s32[4]{0:T(128)} %pad_add_fusion.info, bf16[1,24,256,128]{3,2,1,0:T(8,128)(2,1)} %bitcast.46, bf16[1,24,256,128]{3,2,1,0:T(8,128)(2,1)} %bitcast.50, bf16[1,24,256,128]{3,2,1,0:T(8,128)(2,1)} %bitcast.54, ...), custom_call_target="tpu_custom_call" | custom-call | flops 8000000 | bytes 4718592 | tf_op jit(solution)/shard_map/pack/pallas_call | solution.py:277
  24.9 1.5 collective-permute-done.2.refs_2_
  31.8 1.5 collective-permute-start.7
  33.4 1.0 collective-permute-start.8
  35.2 11.7 %attend.4 = (bf16[1280,256]{1,0:T(8,128)(2,1)}, bf16[1280,256]{1,0:T(8,128)(2,1)}, bf16[1280,256]{1,0:T(8,128)(2,1)}, bf16[1280,256]{1,0:T(8,128)(2,1)}, f32[4,1024,256]{2,1,0:T(8,128)}) custom-call(s32[4]{0:T(128)} %pad_add_fusion.info, ...), custom_call_target="tpu_custom_call", output_to_operand_aliasing={{0}: (12, {}), {1}: (13, {}), {2}: (14, {}), {3}: (15, {})} | custom-call | flops 8000000000 | bytes 1179648 | tf_op jit(solution)/shard_map/attend/pallas_call | solution.py:277
  47.9 1.5 collective-permute-start.13
  49.4 1.0 collective-permute-start.14
  50.4 1.2 collective-permute-done.7.refs_9_
  52.7 27.1 %attend.5 = (bf16[1792,256]{1,0:T(8,128)(2,1)}, bf16[1792,256]{1,0:T(8,128)(2,1)}, bf16[1792,256]{1,0:T(8,128)(2,1)}, bf16[1792,256]{1,0:T(8,128)(2,1)}, f32[4,1024,256]{2,1,0:T(8,128)}) custom-call(s32[4]{0:T(128)} %pad_add_fusion.info, ...), custom_call_target="tpu_custom_call", output_to_operand_aliasing={{0}: (13, {}), {1}: (14, {}), {2}: (15, {}), {3}: (16, {})} | custom-call | flops 24000000000 | bytes 3538944 | tf_op jit(solution)/shard_map/attend/pallas_call | solution.py:277
  79.7 1.5 collective-permute-start.9
  81.8 1.5 collective-permute-start.11
  84.4 34.2 %attend.6 = (bf16[1024,256]{1,0:T(8,128)(2,1)}, bf16[1024,256]{1,0:T(8,128)(2,1)}, bf16[1024,256]{1,0:T(8,128)(2,1)}, bf16[1024,256]{1,0:T(8,128)(2,1)}, f32[4,1024,256]{2,1,0:T(8,128)}) custom-call(s32[4]{0:T(128)} %pad_add_fusion.info, bf16[1280,256]{1,0:T(8,128)(2,1)} %get-tuple-element.65.refs_0_.refs_7_, ...), custom_call_target="tpu_custom_call" | custom-call | flops 32000000000 | bytes 4718592 | tf_op jit(solution)/shard_map/attend/pallas_call | solution.py:277
  118.6 1.5 collective-permute-start.18
  120.7 1.4 collective-permute-start.20
  123.1 34.6 %attend.7 = (bf16[1024,256]{1,0:T(8,128)(2,1)}, bf16[1024,256]{1,0:T(8,128)(2,1)}, bf16[1024,256]{1,0:T(8,128)(2,1)}, bf16[1024,256]{1,0:T(8,128)(2,1)}, bf16[4,...) custom-call(s32[4]{0:T(128)} %pad_add_fusion.info, bf16[1280,256]{1,0:T(8,128)(2,1)} %get-tuple-element.65.refs_0_.refs_7_, ...), custom_call_target="tpu_custom_call" | custom-call | flops 32000000000 | bytes 4718592 | tf_op jit(solution)/shard_map/attend/pallas_call | solution.py:277
  158.9 1.4 collective-permute-start.15
  161.2 1.2 collective-permute-start.17
  163.9 3.5 %collective-permute-start.23 = (bf16[1024,128]{1,0:T(8,128)(2,1)}, bf16[1024,128]{1,0:T(8,128)(2,1)}, u32[]{:S(2)}, u32[]{:S(2)}) collective-permute-start(bf16[1024,128]{1,0:T(8,128)(2,1)} %get-tuple-element.127), channel_id=1, source_target_pairs={{0,16},{4,20},{8,24},{12,28},{16,0},{20,4},{24,8},{28,12},{1,17},{... | collective-permute-start | bytes 786440 | tf_op jit(solution)/shard_map/ppermute | solution.py:424
  167.4 6.5 %collective-permute-done.15.refs_1_ = bf16[1024,256]{1,0:T(8,128)(2,1)S(1)} collective-permute-done((bf16[1024,256]{1,0:T(8,128)(2,1)}, bf16[1024,256]{1,0:T(8,128)(2,1)S(1)}, u32[]{:S(2)}, u32[]{:S(2)}) %collective-permute-start.15) | collective-permute-done | bytes 524320 | tf_op jit(solution)/shard_map/ppermute | solution.py:260
  173.9 1.6 collective-permute-start.22
  175.5 2.8 %unpack.4 = (bf16[1,24,256,128]{3,2,1,0:T(8,128)(2,1)}, bf16[1,24,256,128]{3,2,1,0:T(8,128)(2,1)}, bf16[1,24,256,128]{3,2,1,0:T(8,128)(2,1)}, bf16[1,24,256,128]{3,2,1,0:T(8,128)(2,1)}, f32[8,128]{1,0:T(8,128)}) custom-call(s32[4]{0:T(128)} %pad_add_fusion.info, bf16[1,24,256,128]{3,2,1,0:T(8,128)(2,1)} %bitcast.31, bf16[1,24,256,128]{3,2,1,0:T(8,128)(2,1)} %bitcast.39, ...), custom_call_target="tpu_custom_call" | custom-call | flops 2000000 | bytes 1179648 | tf_op jit(solution)/shard_map/unpack/pallas_call | solution.py:277
  178.3 4.6 %unpack.5 = (bf16[1,24,256,128]{3,2,1,0:T(8,128)(2,1)}, bf16[1,24,256,128]{3,2,1,0:T(8,128)(2,1)}, bf16[1,24,256,128]{3,2,1,0:T(8,128)(2,1)}, bf16[1,24,256,128]{3,2,1,0:T(8,128)(2,1)}, f32[8,128]{1,0:T(8,128)}) custom-call(s32[4]{0:T(128)} %pad_add_fusion.info, ...), custom_call_target="tpu_custom_call", output_to_operand_aliasing={{0}: (7, {}), {1}: (8, {}), {2}: (9, {}), {3}: (10, {})} | custom-call | flops 6000000 | bytes 3538944 | tf_op jit(solution)/shard_map/unpack/pallas_call | solution.py:277
  182.9 5.0 %unpack.6 = (bf16[1,24,256,128]{3,2,1,0:T(8,128)(2,1)}, bf16[1,24,256,128]{3,2,1,0:T(8,128)(2,1)}, bf16[1,24,256,128]{3,2,1,0:T(8,128)(2,1)}, bf16[1,24,256,128]{3,2,1,0:T(8,128)(2,1)}, f32[8,128]{1,0:T(8,128)}) custom-call(s32[4]{0:T(128)} %pad_add_fusion.info, ...), custom_call_target="tpu_custom_call", output_to_operand_aliasing={{0}: (7, {}), {1}: (8, {}), {2}: (9, {}), {3}: (10, {})} | custom-call | flops 8000000 | bytes 4718592 | tf_op jit(solution)/shard_map/unpack/pallas_call | solution.py:277
  188.8 5.0 %unpack.7 = (bf16[1,24,256,128]{3,2,1,0:T(8,128)(2,1)}, bf16[1,24,256,128]{3,2,1,0:T(8,128)(2,1)}, bf16[1,24,256,128]{3,2,1,0:T(8,128)(2,1)}, bf16[1,24,256,128]{3,2,1,0:T(8,128)(2,1)}, f32[8,128]{1,0:T(8,128)}) custom-call(s32[4]{0:T(128)} %pad_add_fusion.info, ...), custom_call_target="tpu_custom_call", output_to_operand_aliasing={{0}: (7, {}), {1}: (8, {}), {2}: (9, {}), {3}: (10, {})} | custom-call | flops 8000000 | bytes 4718592 | tf_op jit(solution)/shard_map/unpack/pallas_call | solution.py:277
  193.8 1.2 slice.47
  195.0 1.9 fusion.3
  197.1 9.1 %all_to_all.5 = bf16[4,256,128]{1,2,0:T(8,128)(2,1)S(1)} all-to-all(bf16[4,256,128]{1,2,0:T(8,128)(2,1)S(1)} %copy.39), channel_id=1, replica_groups=mesh['row'=8,'col'=4] {'col'}, dimensions={0} | all-to-all | bytes 524288 | tf_op jit(solution)/shard_map/all_to_all | solution.py:427
  (85 shorter events, 18.8 us)
Async XLA Ops:
  6.0 18.0 %collective-permute-start = (bf16[768,256]{1,0:T(8,128)(2,1)}, bf16[768,256]{1,0:T(8,128)(2,1)S(1)}, u32[]{:S(2)}, u32[]{:S(2)}) collective-permute-start(bf16[768,256]{1,0:T(8,128)(2,1)} %get-tuple-element.66), channel_id=1, source_target_pairs={{0,1},{1,0},{2,3},{3,2},{4,5},{5,4},{6,7},{7,6},{8,9},{9,8},{10,11... | collective-permute-start | bytes 1179656 | tf_op jit(solution)/shard_map/ppermute | solution.py:260
  6.5 18.4 %collective-permute-start.1 = (bf16[768,256]{1,0:T(8,128)(2,1)}, bf16[768,256]{1,0:T(8,128)(2,1)S(1)}, u32[]{:S(2)}, u32[]{:S(2)}) collective-permute-start(bf16[768,256]{1,0:T(8,128)(2,1)} %get-tuple-element.67), channel_id=1, source_target_pairs={{0,2},{1,3},{2,0},{3,1},{4,6},{5,7},{6,4},{7,5},{8,10},{9,11},{10,... | collective-permute-start | bytes 1179656 | tf_op jit(solution)/shard_map/ppermute | solution.py:260
  8.0 18.4 %collective-permute-start.2 = (bf16[768,256]{1,0:T(8,128)(2,1)}, bf16[768,256]{1,0:T(8,128)(2,1)S(1)}, u32[]{:S(2)}, u32[]{:S(2)}) collective-permute-start(bf16[768,256]{1,0:T(8,128)(2,1)} %get-tuple-element.68), channel_id=1, source_target_pairs={{0,3},{1,2},{2,1},{3,0},{4,7},{5,6},{6,5},{7,4},{8,11},{9,10},{10,... | collective-permute-start | bytes 1179656 | tf_op jit(solution)/shard_map/ppermute | solution.py:260
  24.0 2.4 %copy-start = (bf16[768,256]{1,0:T(8,128)(2,1)}, bf16[768,256]{1,0:T(8,128)(2,1)S(1)}, u32[]{:S(2)}) copy-start(bf16[768,256]{1,0:T(8,128)(2,1)S(1)} %collective-permute-done.refs_0_) | copy-start | bytes 1179652
  24.9 1.5 copy-start.1
  28.2 5.2 %collective-permute-start.3 = (bf16[512,256]{1,0:T(8,128)(2,1)S(1)}, bf16[512,256]{1,0:T(8,128)(2,1)S(1)}, u32[]{:S(2)}, u32[]{:S(2)}) collective-permute-start(bf16[512,256]{1,0:T(8,128)(2,1)S(1)} %slice.36), channel_id=1, source_target_pairs={{0,4},{4,0},{8,12},{12,8},{16,20},{20,16},{24,28},{28,24},{1,5},{5... | collective-permute-start | bytes 786440 | tf_op jit(solution)/shard_map/ppermute | solution.py:263
  29.2 5.2 %collective-permute-start.4 = (bf16[512,256]{1,0:T(8,128)(2,1)S(1)}, bf16[512,256]{1,0:T(8,128)(2,1)S(1)}, u32[]{:S(2)}, u32[]{:S(2)}) collective-permute-start(bf16[512,256]{1,0:T(8,128)(2,1)S(1)} %slice.37), channel_id=1, source_target_pairs={{0,4},{4,0},{8,12},{12,8},{16,20},{20,16},{24,28},{28,24},{1,5},{5... | collective-permute-start | bytes 786440 | tf_op jit(solution)/shard_map/ppermute | solution.py:263
  30.8 3.7 %collective-permute-start.5 = (bf16[512,256]{1,0:T(8,128)(2,1)S(1)}, bf16[512,256]{1,0:T(8,128)(2,1)S(1)}, u32[]{:S(2)}, u32[]{:S(2)}) collective-permute-start(bf16[512,256]{1,0:T(8,128)(2,1)S(1)} %slice.38), channel_id=1, source_target_pairs={{0,4},{4,0},{8,12},{12,8},{16,20},{20,16},{24,28},{28,24},{1,5},{5... | collective-permute-start | bytes 786440 | tf_op jit(solution)/shard_map/ppermute | solution.py:263
  30.8 18.5 %collective-permute-start.6 = (bf16[768,256]{1,0:T(8,128)(2,1)}, bf16[768,256]{1,0:T(8,128)(2,1)S(1)}, u32[]{:S(2)}, u32[]{:S(2)}) collective-permute-start(bf16[768,256]{1,0:T(8,128)(2,1)} %get-tuple-element.78), channel_id=1, source_target_pairs={{0,1},{1,0},{2,3},{3,2},{4,5},{5,4},{6,7},{7,6},{8,9},{9,8},{10,11... | collective-permute-start | bytes 1179656 | tf_op jit(solution)/shard_map/ppermute | solution.py:260
  31.8 19.7 %collective-permute-start.7 = (bf16[768,256]{1,0:T(8,128)(2,1)}, bf16[768,256]{1,0:T(8,128)(2,1)S(1)}, u32[]{:S(2)}, u32[]{:S(2)}) collective-permute-start(bf16[768,256]{1,0:T(8,128)(2,1)} %get-tuple-element.79), channel_id=1, source_target_pairs={{0,2},{1,3},{2,0},{3,1},{4,6},{5,7},{6,4},{7,5},{8,10},{9,11},{10,... | collective-permute-start | bytes 1179656 | tf_op jit(solution)/shard_map/ppermute | solution.py:260
  33.4 18.5 %collective-permute-start.8 = (bf16[768,256]{1,0:T(8,128)(2,1)}, bf16[768,256]{1,0:T(8,128)(2,1)S(1)}, u32[]{:S(2)}, u32[]{:S(2)}) collective-permute-start(bf16[768,256]{1,0:T(8,128)(2,1)} %get-tuple-element.80), channel_id=1, source_target_pairs={{0,3},{1,2},{2,1},{3,0},{4,7},{5,6},{6,5},{7,4},{8,11},{9,10},{10,... | collective-permute-start | bytes 1179656 | tf_op jit(solution)/shard_map/ppermute | solution.py:260
  46.9 34.9 %collective-permute-start.12 = (bf16[1280,256]{1,0:T(8,128)(2,1)}, bf16[1280,256]{1,0:T(8,128)(2,1)S(1)}, u32[]{:S(2)}, u32[]{:S(2)}) collective-permute-start(bf16[1280,256]{1,0:T(8,128)(2,1)} %get-tuple-element.93), channel_id=1, source_target_pairs={{0,1},{1,0},{2,3},{3,2},{4,5},{5,4},{6,7},{7,6},{8,9},{9,8},{10,11... | collective-permute-start | bytes 1966088 | tf_op jit(solution)/shard_map/ppermute | solution.py:260
  47.9 35.4 %collective-permute-start.13 = (bf16[1280,256]{1,0:T(8,128)(2,1)}, bf16[1280,256]{1,0:T(8,128)(2,1)S(1)}, u32[]{:S(2)}, u32[]{:S(2)}) collective-permute-start(bf16[1280,256]{1,0:T(8,128)(2,1)} %get-tuple-element.94), channel_id=1, source_target_pairs={{0,2},{1,3},{2,0},{3,1},{4,6},{5,7},{6,4},{7,5},{8,10},{9,11},{10,... | collective-permute-start | bytes 1966088 | tf_op jit(solution)/shard_map/ppermute | solution.py:260
  49.4 2.6 %copy-start.15 = (bf16[768,256]{1,0:T(8,128)(2,1)}, bf16[768,256]{1,0:T(8,128)(2,1)S(1)}, u32[]{:S(2)}) copy-start(bf16[768,256]{1,0:T(8,128)(2,1)S(1)} %collective-permute-done.6.refs_8_) | copy-start | bytes 1179652
  49.4 33.9 %collective-permute-start.14 = (bf16[1280,256]{1,0:T(8,128)(2,1)}, bf16[1280,256]{1,0:T(8,128)(2,1)S(1)}, u32[]{:S(2)}, u32[]{:S(2)}) collective-permute-start(bf16[1280,256]{1,0:T(8,128)(2,1)} %get-tuple-element.95), channel_id=1, source_target_pairs={{0,3},{1,2},{2,1},{3,0},{4,7},{5,6},{6,5},{7,4},{8,11},{9,10},{10,... | collective-permute-start | bytes 1966088 | tf_op jit(solution)/shard_map/ppermute | solution.py:260
  79.7 41.0 %collective-permute-start.9 = (bf16[1792,256]{1,0:T(8,128)(2,1)}, bf16[1792,256]{1,0:T(8,128)(2,1)S(1)}, u32[]{:S(2)}, u32[]{:S(2)}) collective-permute-start(bf16[1792,256]{1,0:T(8,128)(2,1)} %get-tuple-element.89), channel_id=1, source_target_pairs={{0,1},{1,0},{2,3},{3,2},{4,5},{5,4},{6,7},{7,6},{8,9},{9,8},{10,11... | collective-permute-start | bytes 2752520 | tf_op jit(solution)/shard_map/ppermute | solution.py:260
  81.2 40.9 %collective-permute-start.10 = (bf16[1792,256]{1,0:T(8,128)(2,1)}, bf16[1792,256]{1,0:T(8,128)(2,1)S(1)}, u32[]{:S(2)}, u32[]{:S(2)}) collective-permute-start(bf16[1792,256]{1,0:T(8,128)(2,1)} %get-tuple-element.90), channel_id=1, source_target_pairs={{0,2},{1,3},{2,0},{3,1},{4,6},{5,7},{6,4},{7,5},{8,10},{9,11},{10,... | collective-permute-start | bytes 2752520 | tf_op jit(solution)/shard_map/ppermute | solution.py:260
  81.8 1.5 copy-start.9
  81.8 41.2 %collective-permute-start.11 = (bf16[1792,256]{1,0:T(8,128)(2,1)}, bf16[1792,256]{1,0:T(8,128)(2,1)}, u32[]{:S(2)}, u32[]{:S(2)}) collective-permute-start(bf16[1792,256]{1,0:T(8,128)(2,1)} %get-tuple-element.91), channel_id=1, source_target_pairs={{0,3},{1,2},{2,1},{3,0},{4,7},{5,6},{6,5},{7,4},{8,11},{9,10},{10,... | collective-permute-start | bytes 2752520 | tf_op jit(solution)/shard_map/ppermute | solution.py:260
  118.6 39.2 %collective-permute-start.18 = (bf16[1024,256]{1,0:T(8,128)(2,1)}, bf16[1024,256]{1,0:T(8,128)(2,1)S(1)}, u32[]{:S(2)}, u32[]{:S(2)}) collective-permute-start(bf16[1024,256]{1,0:T(8,128)(2,1)} %get-tuple-element.103), channel_id=1, source_target_pairs={{0,1},{1,0},{2,3},{3,2},{4,5},{5,4},{6,7},{7,6},{8,9},{9,8},{10,11... | collective-permute-start | bytes 1572872 | tf_op jit(solution)/shard_map/ppermute | solution.py:260
  120.1 37.6 %collective-permute-start.19 = (bf16[1024,256]{1,0:T(8,128)(2,1)}, bf16[1024,256]{1,0:T(8,128)(2,1)S(1)}, u32[]{:S(2)}, u32[]{:S(2)}) collective-permute-start(bf16[1024,256]{1,0:T(8,128)(2,1)} %get-tuple-element.104), channel_id=1, source_target_pairs={{0,2},{1,3},{2,0},{3,1},{4,6},{5,7},{6,4},{7,5},{8,10},{9,11},{10,... | collective-permute-start | bytes 1572872 | tf_op jit(solution)/shard_map/ppermute | solution.py:260
  120.7 2.3 %copy-start.7 = (bf16[1792,256]{1,0:T(8,128)(2,1)}, bf16[1792,256]{1,0:T(8,128)(2,1)S(1)}, u32[]{:S(2)}) copy-start(bf16[1792,256]{1,0:T(8,128)(2,1)S(1)} %collective-permute-done.9.refs_8_.refs_1_) | copy-start | bytes 2752516
  120.7 37.1 %collective-permute-start.20 = (bf16[1024,256]{1,0:T(8,128)(2,1)}, bf16[1024,256]{1,0:T(8,128)(2,1)S(1)}, u32[]{:S(2)}, u32[]{:S(2)}) collective-permute-start(bf16[1024,256]{1,0:T(8,128)(2,1)} %get-tuple-element.105), channel_id=1, source_target_pairs={{0,3},{1,2},{2,1},{3,0},{4,7},{5,6},{6,5},{7,4},{8,11},{9,10},{10,... | collective-permute-start | bytes 1572872 | tf_op jit(solution)/shard_map/ppermute | solution.py:260
  158.9 3.5 %copy-start.6 = (bf16[4,1024,128]{2,1,0:T(8,128)(2,1)S(1)}, bf16[4,1024,128]{2,1,0:T(8,128)(2,1)}, u32[]{:S(2)}) copy-start(bf16[4,1024,128]{2,1,0:T(8,128)(2,1)} %get-tuple-element.122) | copy-start | bytes 3145732
  158.9 3.5 %collective-permute-start.21 = (bf16[4,1024,128]{2,1,0:T(8,128)(2,1)}, bf16[4,1024,128]{2,1,0:T(8,128)(2,1)S(1)}, u32[]{:S(2)}, u32[]{:S(2)}) collective-permute-start(bf16[4,1024,128]{2,1,0:T(8,128)(2,1)} %hold.5), channel_id=1, source_target_pairs={{0,4},{4,0},{8,12},{12,8},{16,20},{20,16},{24,28},{28,24},{1,5},{5... | collective-permute-start | bytes 3145736 | tf_op jit(solution)/shard_map/ppermute | solution.py:263
  158.9 14.9 %collective-permute-start.15 = (bf16[1024,256]{1,0:T(8,128)(2,1)}, bf16[1024,256]{1,0:T(8,128)(2,1)S(1)}, u32[]{:S(2)}, u32[]{:S(2)}) collective-permute-start(bf16[1024,256]{1,0:T(8,128)(2,1)} %get-tuple-element.99), channel_id=1, source_target_pairs={{0,1},{1,0},{2,3},{3,2},{4,5},{5,4},{6,7},{7,6},{8,9},{9,8},{10,11... | collective-permute-start | bytes 1572872 | tf_op jit(solution)/shard_map/ppermute | solution.py:260
  160.4 27.5 %collective-permute-start.16 = (bf16[1024,256]{1,0:T(8,128)(2,1)}, bf16[1024,256]{1,0:T(8,128)(2,1)S(1)}, u32[]{:S(2)}, u32[]{:S(2)}) collective-permute-start(bf16[1024,256]{1,0:T(8,128)(2,1)} %get-tuple-element.100), channel_id=1, source_target_pairs={{0,2},{1,3},{2,0},{3,1},{4,6},{5,7},{6,4},{7,5},{8,10},{9,11},{10,... | collective-permute-start | bytes 1572872 | tf_op jit(solution)/shard_map/ppermute | solution.py:260
  161.2 26.7 %collective-permute-start.17 = (bf16[1024,256]{1,0:T(8,128)(2,1)}, bf16[1024,256]{1,0:T(8,128)(2,1)S(1)}, u32[]{:S(2)}, u32[]{:S(2)}) collective-permute-start(bf16[1024,256]{1,0:T(8,128)(2,1)} %get-tuple-element.101), channel_id=1, source_target_pairs={{0,3},{1,2},{2,1},{3,0},{4,7},{5,6},{6,5},{7,4},{8,11},{9,10},{10,... | collective-permute-start | bytes 1572872 | tf_op jit(solution)/shard_map/ppermute | solution.py:260
  163.4 31.6 %collective-permute-start.24 = (bf16[1024,128]{1,0:T(8,128)(2,1)}, bf16[1024,128]{1,0:T(8,128)(2,1)}, u32[]{:S(2)}, u32[]{:S(2)}) collective-permute-start(bf16[1024,128]{1,0:T(8,128)(2,1)} %get-tuple-element.126), channel_id=1, source_target_pairs={{0,24},{4,28},{8,16},{12,20},{16,8},{20,12},{24,0},{28,4},{1,25},{... | collective-permute-start | bytes 786440 | tf_op jit(solution)/shard_map/ppermute | solution.py:424
  163.9 31.1 %collective-permute-start.23 = (bf16[1024,128]{1,0:T(8,128)(2,1)}, bf16[1024,128]{1,0:T(8,128)(2,1)}, u32[]{:S(2)}, u32[]{:S(2)}) collective-permute-start(bf16[1024,128]{1,0:T(8,128)(2,1)} %get-tuple-element.127), channel_id=1, source_target_pairs={{0,16},{4,20},{8,24},{12,28},{16,0},{20,4},{24,8},{28,12},{1,17},{... | collective-permute-start | bytes 786440 | tf_op jit(solution)/shard_map/ppermute | solution.py:424
  173.9 4.4 %copy-start.12 = (bf16[1024,256]{1,0:T(8,128)(2,1)}, bf16[1024,256]{1,0:T(8,128)(2,1)S(1)}, u32[]{:S(2)}) copy-start(bf16[1024,256]{1,0:T(8,128)(2,1)S(1)} %collective-permute-done.15.refs_1_) | copy-start | bytes 1572868
  173.9 21.1 %collective-permute-start.22 = (bf16[1024,128]{1,0:T(8,128)(2,1)S(1)}, bf16[1024,128]{1,0:T(8,128)(2,1)}, u32[]{:S(2)}, u32[]{:S(2)}) collective-permute-start(bf16[1024,128]{1,0:T(8,128)(2,1)S(1)} %get-tuple-element.125), channel_id=1, source_target_pairs={{0,8},{4,12},{8,0},{12,4},{16,24},{20,28},{24,16},{28,20},{1,9},{5... | collective-permute-start | bytes 786440 | tf_op jit(solution)/shard_map/ppermute | solution.py:424
  (14 other events, 12.4 us)
where the time goes:
time: 210 us; the launch traced here: 207 us
  Pallas kernels  144 us (69%)
  starting transfers between devices  27.4 us (13%)
  waiting for transfers between devices  11.3 us (5%)
  local copies, waits for them, and re-layouts  9.77 us (5%)
  blocking collectives  9.1 us (4%)
  other arithmetic  4.34 us (2%)
    pallas_call x12, Pallas kernels, call(): pl.pallas_call(kernel, grid_spec=pltpu.PrefetchScalarGridSpec(num_scalar_...  144 us
    ppermute x18, starting transfers between devices, exchange(): lax.ppermute(blocks[step], 'col', pairs[step])  21.1 us
    ppermute x18, waiting for transfers between devices, exchange(): lax.ppermute(blocks[step], 'col', pairs[step])  11.3 us
    all_to_all x1, blocking collectives, on_device(): lax.all_to_all(total, 'col', split_axis=0, concat_axis=0, tiled=True)  9.1 us
    ppermute x3, starting transfers between devices, on_device(): shares.append(lax.ppermute(share, 'row', pairs) if step else share)  5.55 us
    unnamed x42, local copies, waits for them, and re-layouts  5.54 us
  transfers between devices with their start and end apart: 25, of which 6 were waited for; matrix products, arithmetic and copies ran while one was open for 2% of the time, Pallas kernels for 67%

commit v1 on v0

--- a/solution.py
+++ b/solution.py
@@ -22,26 +22,35 @@
     return jnp.bitwise_xor(me, step)
 
 
+def selection(groups, c, me, shape, group):
+    place = lax.broadcasted_iota(jnp.int32, shape, 0)
+    channel = lax.broadcasted_iota(jnp.int32, shape, 1)
+    peer = peer_of(me, place // c)
+    found = jnp.logical_and(peer % groups == group, channel == peer // groups * c + place % c)
+    return jnp.where(found, 1.0, 0.0).astype(jnp.bfloat16)
+
+
 def pack_kernel(heads, groups, with_bias, info, q_ref, k_ref, v_ref, g_ref, o_ref, *refs):
     n_col = heads * groups
-    outs, turned = refs[-1 - n_col : -1], refs[-1]
+    outs = refs[-n_col:]
     me = info[1]
     count, _, channels = q_ref.shape[1:]
     c = channels // heads
     lines = count * PIECES * c
+    selections = [selection(groups, c, me, (n_col * c, channels), g) for g in range(groups)]
     for i in range(count):
+        turned = [0.0] * PIECES
         for g in range(groups):
             gated = o_ref[g, i].astype(jnp.float32) * jax.nn.sigmoid(g_ref[g, i].astype(jnp.float32))
             pieces = (q_ref[g, i], k_ref[g, i], v_ref[g, i], gated.astype(jnp.bfloat16))
             for piece, x in enumerate(pieces):
-                turned[g, i, piece] = x.T
+                turned[piece] += dot(selections[g], x, ((1,), (1,)))
         for step in range(n_col):
-            peer = peer_of(me, step)
-            head = pl.multiple_of(peer // groups * c, c)
             base = outs[step].shape[0] - lines
             for piece in range(PIECES):
                 at = base + (i * PIECES + piece) * c
-                outs[step][at : at + c, :] = turned[peer % groups, i, piece, pl.ds(head, c), :]
+                block = turned[piece][step * c : (step + 1) * c]
+                outs[step][at : at + c, :] = block.astype(jnp.bfloat16)
     if with_bias:
         for step in range(n_col):
             base = outs[step].shape[0] - lines
@@ -54,8 +63,11 @@
     ins, (dq, dk, dv, dg, token, whole) = refs[:n_col], refs[-6:]
     token[...] = jnp.zeros_like(token)
     me = info[1]
-    count, _, channels = g_ref.shape[1:]
+    count, blk, channels = g_ref.shape[1:]
     c = channels // heads
+    square = (blk, blk)
+    same = lax.broadcasted_iota(jnp.int32, square, 0) == lax.broadcasted_iota(jnp.int32, square, 1)
+    same = jnp.where(same, 1.0, 0.0).astype(jnp.bfloat16)
     for i in range(count):
         for step in range(n_col):
             peer = peer_of(me, step)
@@ -64,12 +76,13 @@
                 at = (i * PIECES + piece) * c
                 whole[peer % groups, i, piece, pl.ds(head, c), :] = ins[step][at : at + c, :]
         for g in range(groups):
-            dq[g, i] = whole[g, i, 0].T
-            dk[g, i] = whole[g, i, 1].T
-            dv[g, i] = whole[g, i, 2].T
-            attended = whole[g, i, 3].T.astype(jnp.float32)
+            turned = [dot(same, whole[g, i, piece], ((1,), (1,))) for piece in range(PIECES)]
+            dq[g, i] = turned[0].astype(jnp.bfloat16)
+            dk[g, i] = turned[1].astype(jnp.bfloat16)
+            dv[g, i] = turned[2].astype(jnp.bfloat16)
             s = jax.nn.sigmoid(g_ref[g, i].astype(jnp.float32))
-            dg[g, i] = (o_ref[g, i].astype(jnp.float32) * attended * s * (1.0 - s)).astype(jnp.bfloat16)
+            up = o_ref[g, i].astype(jnp.float32)
+            dg[g, i] = (up * turned[3] * s * (1.0 - s)).astype(jnp.bfloat16)
 
 
 def woven(*queues):
@@ -81,7 +94,7 @@
 def attention_kernel(n_col, together, c, scaling, first, last, info, *refs):
     bias_in, ins, refs = refs[: 2 * n_col - 1], refs[2 * n_col - 1 : 3 * n_col - 1], refs[3 * n_col - 1 :]
     scratch, refs = refs[-14:], refs[:-14]
-    bias, total_s, q_s, g_s, k_s, v_s, k_turned, v_turned, dq_s, at_s, dkv, logits, weights, grads = scratch
+    bias, total_s, q_s, g_s, k_s, v_s, k_turned, v_turned, dq_s, at_s, dkv, logits, both, sides = scratch
     if not first:
         total_in = refs[0]
     totals = refs[-2:] if last else refs[-1:]
@@ -114,6 +127,7 @@
             k_s[r, 2 * c :, :] = jnp.where(mask, MASKED, 0.0).astype(jnp.bfloat16)
             v_s[r, c:, :] = jnp.ones((deep - c, n), jnp.bfloat16)
             q_s[r, :, 2 * c :, :] = jnp.ones((n_col, deep - 2 * c, blk), jnp.bfloat16)
+        sides[...] = jnp.zeros_like(sides)
 
     def rows_of(r, piece):
         at = (r * PIECES + piece) * c
@@ -135,7 +149,13 @@
     for r in some:
         k_turned[r] = k_s[r].T
         v_turned[r] = v_s[r].T
-    tops, scaled, scales = {}, {}, {}
+    tops, scales = {}, {}
+
+    def gradient(r):
+        return slice(2 * r * blk, (2 * r + 1) * blk)
+
+    def weight(r):
+        return slice((2 * r + 1) * blk, (2 * r + 2) * blk)
 
     def score(jb, r, t):
         part = dot(k_turned[r, t : t + tile, :], q_s[r, jb], ((1,), (0,))) + bias[jb, t : t + tile, :]
@@ -147,10 +167,10 @@
         if t == 0:
             tops[jb, r] = jnp.max(tops[jb, r], axis=0, keepdims=True)
         part = jnp.exp2(logits[jb % 2, r, t : t + tile, :] - tops[jb, r])
-        weights[jb % 2, r, t : t + tile, :] = part.astype(jnp.bfloat16)
+        both[jb % 2, t : t + tile, weight(r)] = part.astype(jnp.bfloat16)
 
     def attend(jb, r):
-        summed = dot(v_s[r, : c + 16, :], weights[jb % 2, r], ((1,), (0,)))
+        summed = dot(v_s[r, : c + 16, :], both[jb % 2, :, weight(r)], ((1,), (0,)))
         inverse = 1.0 / summed[c : c + 1, :]
         attended = summed[:c, :] * inverse
         at_s[r, jb] = attended.astype(jnp.bfloat16)
@@ -159,31 +179,27 @@
         high = row_dot.astype(jnp.bfloat16).astype(jnp.float32)
         rows = lax.broadcasted_iota(jnp.int32, (deep - c, blk), 0)
         tail = jnp.where(rows == 0, high, jnp.where(rows == 1, row_dot - high, 0.0))
-        scaled[jb, r] = (g * inverse).astype(jnp.bfloat16)
-        scales[jb, r] = jnp.concatenate([scaled[jb, r], tail.astype(jnp.bfloat16)], axis=0)
+        scaled = (g * inverse).astype(jnp.bfloat16)
+        scales[jb, r] = jnp.concatenate([scaled, tail.astype(jnp.bfloat16)], axis=0)
+        sides[jb % 2, 2 * r * c : (2 * r + 1) * c, gradient(r)] = q_s[r, jb, :c, :]
+        sides[jb % 2, (2 * r + 1) * c : (2 * r + 2) * c, weight(r)] = scaled
 
     def back(jb, t):
         added = total[jb, t : t + tile, :]
         for r in some:
             grad = dot(v_turned[r, t : t + tile, :], scales[jb, r], ((1,), (0,)))
-            grad = grad * weights[jb % 2, r, t : t + tile, :].astype(jnp.float32)
+            grad = grad * both[jb % 2, t : t + tile, weight(r)].astype(jnp.float32)
             added = added + grad
-            grads[jb % 2, r, t : t + tile, :] = grad.astype(jnp.bfloat16)
+            both[jb % 2, t : t + tile, gradient(r)] = grad.astype(jnp.bfloat16)
         total[jb, t : t + tile, :] = added
 
     def query_grad(jb, r):
-        dq_s[r, jb] = (dot(k_s[r, :c, :], grads[jb % 2, r], ((1,), (0,))) * scaling).astype(jnp.bfloat16)
-
-    def add_to(at, r, jb, part):
-        if jb:
-            part = part + dkv[r, at : at + c, :]
-        dkv[r, at : at + c, :] = part
-
-    def key_grad(jb, r):
-        add_to(0, r, jb, dot(q_s[r, jb, :c, :], grads[jb % 2, r], ((1,), (1,))))
-
-    def value_grad(jb, r):
-        add_to(c, r, jb, dot(scaled[jb, r], weights[jb % 2, r], ((1,), (1,))))
+        part = dot(k_s[r, :c, :], both[jb % 2, :, gradient(r)], ((1,), (0,)))
+        dq_s[r, jb] = (part * scaling).astype(jnp.bfloat16)
+
+    def key_value_grad(jb, t):
+        part = dot(both[jb % 2, t : t + tile, :], sides[jb % 2], ((1,), (1,)))
+        dkv[t : t + tile, :] = part + dkv[t : t + tile, :] if jb else part
 
     def each(step, jb, *ranges):
         if not 0 <= jb < n_col:
@@ -191,7 +207,7 @@
         return [functools.partial(step, jb, *at) for at in itertools.product(*ranges)]
 
     def finish(jb):
-        return each(value_grad, jb, some) + each(query_grad, jb, some) + each(key_grad, jb, some)
+        return each(query_grad, jb, some) + each(key_value_grad, jb, tiles)
 
     woven(each(score, 0, some, tiles))
     for jb in range(n_col):
@@ -200,13 +216,14 @@
         woven(each(back, jb, tiles), each(score, jb + 1, some, tiles[len(tiles) // 2 :]))
     woven(finish(n_col - 1))
 
-    for r in some:
-        for step in range(n_col):
-            jb = peer_of(me, step)
-            span = pl.ds(pl.multiple_of(jb * blk, blk), blk)
+    for step in range(n_col):
+        jb = peer_of(me, step)
+        turned = dkv[pl.ds(pl.multiple_of(jb * blk, blk), blk), :].T
+        for r in some:
+            at = 2 * r * c
             outs[step][rows_of(r, 0), :] = dq_s[r, jb]
-            outs[step][rows_of(r, 1), :] = (dkv[r, :c, span] * (1.0 / LOG2E)).astype(jnp.bfloat16)
-            outs[step][rows_of(r, 2), :] = dkv[r, c:, span].astype(jnp.bfloat16)
+            outs[step][rows_of(r, 1), :] = (turned[at : at + c] * (1.0 / LOG2E)).astype(jnp.bfloat16)
+            outs[step][rows_of(r, 2), :] = turned[at + c : at + 2 * c].astype(jnp.bfloat16)
             outs[step][rows_of(r, 3), :] = at_s[r, jb]
 
     if last:
@@ -317,7 +334,7 @@
             operands,
             [part(x + step * lines, 0) for x in ahead],
             [jax.ShapeDtypeStruct((x + size, blk), jnp.bfloat16) for x in ahead],
-            [pltpu.VMEM((groups, step, PIECES, channels, blk), jnp.bfloat16)],
+            [],
             {},
         )
 
@@ -367,10 +384,10 @@
                 scratch(n, deep),
                 scratch(n_col, c, blk),
                 scratch(n_col, c, blk),
-                scratch(2 * c, n, dtype=jnp.float32),
+                pltpu.VMEM((n, 2 * per * c), jnp.float32),
                 pltpu.VMEM((2, per, n, blk), jnp.float32),
-                pltpu.VMEM((2, per, n, blk), jnp.bfloat16),
-                pltpu.VMEM((2, per, n, blk), jnp.bfloat16),
+                pltpu.VMEM((2, n, 2 * per * blk), jnp.bfloat16),
+                pltpu.VMEM((2, 2 * per * c, 2 * per * blk), jnp.bfloat16),
             ],
             aliases,
         )
@@ -410,8 +427,10 @@
         room = packed[m + 2] if m + 2 < chunks else None
         results, totals = attend(m, totals[0], tables, arrived[m], room)
         arrived.append(exchange(results))
+    tokens = []
     for m in range(chunks):
         *grads, token = unpack(m, arrived[m + 2], grads)
+        tokens.append(token)
 
     mine, others = totals
     (others,) = hold([others], arrived[chunks][1:])
@@ -422,7 +441,7 @@
         pairs = [(r, r ^ (2 * step)) for r in range(n_row)]
         share = share.astype(jnp.bfloat16)
         shares.append(lax.ppermute(share, "row", pairs) if step else share)
-    total = sum(x.astype(jnp.float32) for x in shares) + token[0, 0]
+    total = sum(x.astype(jnp.float32) for x in shares) + tokens[-2][0, 0]
     total = total.astype(jnp.bfloat16).reshape(n_col, blk, width)
     total = lax.all_to_all(total, "col", split_axis=0, concat_axis=0, tiled=True)
     total = jnp.sum(total.reshape(heads, groups, blk, width).astype(jnp.float32), axis=1)

time: 210 us -> 222 us (1.057)
  waiting for transfers between devices: 11.3 us -> 20.5 us
  blocking collectives: 9.1 us -> 0 us
  Pallas kernels: 144 us -> 153 us
  starting transfers between devices: 27.4 us -> 31.2 us
    ppermute x3, waiting for transfers between devices: 0.01 us -> 14.4 us  [on_device(): shares.append(lax.ppermute(share, 'row', pairs) if step else share)]
    pallas_call x12, Pallas kernels: 144 us -> 153 us  [call(): pl.pallas_call(kernel, grid_spec=pltpu.PrefetchScalarGridSpec(num_scalar_...]
    all_to_all x1 -> x0, blocking collectives: 9.1 us -> none  [on_device(): lax.all_to_all(total, 'col', split_axis=0, concat_axis=0, tiled=True)]
    ppermute x18, waiting for transfers between devices: 11.3 us -> 3.2 us  [exchange(): lax.ppermute(blocks[step], 'col', pairs[step])]
    all_to_all x0 -> x1, starting transfers between devices: none -> 5.34 us  [on_device(): lax.all_to_all(total, 'col', split_axis=0, concat_axis=0, tiled=True)]
    ppermute x4, waiting for transfers between devices: 0.01 us -> 2.88 us  [swap(): return lax.ppermute(x, 'row', [(r, r ^ 1) for r in range(n_row)])]
    unnamed x42 -> x40, local copies, waits for them, and re-layouts: 5.54 us -> 6.34 us
  transfers between devices with their start and end apart: 25 -> 26, of which waited for: 6 -> 6; matrix products, arithmetic and copies ran while one was open for 2% -> 3% of each run, Pallas kernels for 67% -> 67%
where the time goes in v1:
time: 222 us; the launch traced here: 221 us
  Pallas kernels  153 us (69%)
  starting transfers between devices  31.2 us (14%)
  waiting for transfers between devices  20.5 us (9%)
  local copies, waits for them, and re-layouts  11.3 us (5%)
  other arithmetic  3.49 us (2%)
    pallas_call x12, Pallas kernels, call(): pl.pallas_call(kernel, grid_spec=pltpu.PrefetchScalarGridSpec(num_scalar_...  153 us
    ppermute x18, starting transfers between devices, exchange(): lax.ppermute(blocks[step], 'col', pairs[step])  21.1 us
    ppermute x3, waiting for transfers between devices, on_device(): shares.append(lax.ppermute(share, 'row', pairs) if step else share)  14.4 us
    unnamed x40, local copies, waits for them, and re-layouts  6.34 us
    all_to_all x1, starting transfers between devices, on_device(): lax.all_to_all(total, 'col', split_axis=0, concat_axis=0, tiled=True)  5.34 us
  transfers between devices with their start and end apart: 26, of which 6 were waited for; matrix products, arithmetic and copies ran while one was open for 3% of the time, Pallas kernels for 67%

profile of v1, /device:TPU:18, one launch (start us, length us, event | category | flops | bytes accessed | tf_op | source)
XLA Modules:
  0.0 221.0 jit_solution(3640214101942282095)
XLA Ops:
  1.9 4.1 %pack.4 = (bf16[1280,256]{1,0:T(8,128)(2,1)}, bf16[768,256]{1,0:T(8,128)(2,1)}, bf16[768,256]{1,0:T(8,128)(2,1)}, bf16[768,256]{1,0:T(8,128)(2,1)}) custom-call(s32[4]{0:T(128)} %pad_add_fusion.info, bf16[1,24,256,128]{3,2,1,0:T(8,128)(2,1)} %bitcast.43, bf16[1,24,256,128]{3,2,1,0:T(8,128)(2,1)} %bitcast.47, bf16[1,24,256,128]{3,2,1,0:T(8,128)(2,1)} %bitcast.51, ...), custom_call_target="tpu_custom_call" | custom-call | flops 2000000 | bytes 1179648 | tf_op jit(solution)/shard_map/pack/pallas_call | solution.py:294
  6.5 1.5 collective-permute-start.1
  8.1 1.4 collective-permute-start.2
  9.5 4.8 %pack.5 = (bf16[768,256]{1,0:T(8,128)(2,1)}, bf16[768,256]{1,0:T(8,128)(2,1)}, bf16[768,256]{1,0:T(8,128)(2,1)}, bf16[768,256]{1,0:T(8,128)(2,1)}) custom-call(s32[4]{0:T(128)} %pad_add_fusion.info, bf16[1,24,256,128]{3,2,1,0:T(8,128)(2,1)} %bitcast.44, bf16[1,24,256,128]{3,2,1,0:T(8,128)(2,1)} %bitcast.48, bf16[1,24,256,128]{3,2,1,0:T(8,128)(2,1)} %bitcast.52, ...), custom_call_target="tpu_custom_call" | custom-call | flops 6000000 | bytes 3538944 | tf_op jit(solution)/shard_map/pack/pallas_call | solution.py:294
  14.2 5.2 %pack.6 = (bf16[1280,256]{1,0:T(8,128)(2,1)}, bf16[1280,256]{1,0:T(8,128)(2,1)}, bf16[1280,256]{1,0:T(8,128)(2,1)}, bf16[1280,256]{1,0:T(8,128)(2,1)}) custom-call(s32[4]{0:T(128)} %pad_add_fusion.info, bf16[1,24,256,128]{3,2,1,0:T(8,128)(2,1)} %bitcast.45, bf16[1,24,256,128]{3,2,1,0:T(8,128)(2,1)} %bitcast.49, bf16[1,24,256,128]{3,2,1,0:T(8,128)(2,1)} %bitcast.53, ...), custom_call_target="tpu_custom_call" | custom-call | flops 8000000 | bytes 4718592 | tf_op jit(solution)/shard_map/pack/pallas_call | solution.py:294
  19.4 5.1 %pack.7 = (bf16[1792,256]{1,0:T(8,128)(2,1)}, bf16[1792,256]{1,0:T(8,128)(2,1)}, bf16[1792,256]{1,0:T(8,128)(2,1)}, bf16[1792,256]{1,0:T(8,128)(2,1)}) custom-call(s32[4]{0:T(128)} %pad_add_fusion.info, bf16[1,24,256,128]{3,2,1,0:T(8,128)(2,1)} %bitcast.46, bf16[1,24,256,128]{3,2,1,0:T(8,128)(2,1)} %bitcast.50, bf16[1,24,256,128]{3,2,1,0:T(8,128)(2,1)} %bitcast.54, ...), custom_call_target="tpu_custom_call" | custom-call | flops 8000000 | bytes 4718592 | tf_op jit(solution)/shard_map/pack/pallas_call | solution.py:294
  24.9 1.5 collective-permute-done.2.refs_2_
  30.8 1.0 collective-permute-start.6
  31.8 1.5 collective-permute-start.7
  33.4 1.0 collective-permute-start.8
  35.2 12.0 %attend.4 = (bf16[1280,256]{1,0:T(8,128)(2,1)}, bf16[1280,256]{1,0:T(8,128)(2,1)}, bf16[1280,256]{1,0:T(8,128)(2,1)}, bf16[1280,256]{1,0:T(8,128)(2,1)}, f32[4,1024,256]{2,1,0:T(8,128)}) custom-call(s32[4]{0:T(128)} %pad_add_fusion.info, ...), custom_call_target="tpu_custom_call", output_to_operand_aliasing={{0}: (12, {}), {1}: (13, {}), {2}: (14, {}), {3}: (15, {})} | custom-call | flops 8000000000 | bytes 1179648 | tf_op jit(solution)/shard_map/attend/pallas_call | solution.py:294
  48.1 1.5 collective-permute-start.13
  49.6 1.0 collective-permute-start.14
  52.7 29.3 %attend.5 = (bf16[1792,256]{1,0:T(8,128)(2,1)}, bf16[1792,256]{1,0:T(8,128)(2,1)}, bf16[1792,256]{1,0:T(8,128)(2,1)}, bf16[1792,256]{1,0:T(8,128)(2,1)}, f32[4,1024,256]{2,1,0:T(8,128)}) custom-call(s32[4]{0:T(128)} %pad_add_fusion.info, ...), custom_call_target="tpu_custom_call", output_to_operand_aliasing={{0}: (13, {}), {1}: (14, {}), {2}: (15, {}), {3}: (16, {})} | custom-call | flops 24000000000 | bytes 3538944 | tf_op jit(solution)/shard_map/attend/pallas_call | solution.py:294
  82.0 1.5 collective-permute-start.9
  84.1 1.5 collective-permute-start.11
  86.6 37.0 %attend.6 = (bf16[1024,256]{1,0:T(8,128)(2,1)}, bf16[1024,256]{1,0:T(8,128)(2,1)}, bf16[1024,256]{1,0:T(8,128)(2,1)}, bf16[1024,256]{1,0:T(8,128)(2,1)}, f32[4,1024,256]{2,1,0:T(8,128)}) custom-call(s32[4]{0:T(128)} %pad_add_fusion.info, bf16[1280,256]{1,0:T(8,128)(2,1)} %get-tuple-element.65.refs_0_.refs_7_, ...), custom_call_target="tpu_custom_call" | custom-call | flops 32000000000 | bytes 4718592 | tf_op jit(solution)/shard_map/attend/pallas_call | solution.py:294
  123.6 1.5 collective-permute-start.18
  125.7 1.5 collective-permute-start.20
  128.1 36.8 %attend.7 = (bf16[1024,256]{1,0:T(8,128)(2,1)}, bf16[1024,256]{1,0:T(8,128)(2,1)}, bf16[1024,256]{1,0:T(8,128)(2,1)}, bf16[1024,256]{1,0:T(8,128)(2,1)}, bf16[4,...) custom-call(s32[4]{0:T(128)} %pad_add_fusion.info, bf16[1280,256]{1,0:T(8,128)(2,1)} %get-tuple-element.65.refs_0_.refs_7_, ...), custom_call_target="tpu_custom_call" | custom-call | flops 32000000000 | bytes 4718592 | tf_op jit(solution)/shard_map/attend/pallas_call | solution.py:294
  166.1 2.9 %collective-permute-done.21 = bf16[4,1024,128]{2,1,0:T(8,128)(2,1)S(1)} collective-permute-done((bf16[4,1024,128]{2,1,0:T(8,128)(2,1)}, bf16[4,1024,128]{2,1,0:T(8,128)(2,1)S(1)}, u32[]{:S(2)}, u32[]{:S(2)}) %collective-permute-start.21) | collective-permute-done | bytes 1048608 | tf_op jit(solution)/shard_map/ppermute | solution.py:280
  169.7 3.5 %collective-permute-start.23 = (bf16[1024,128]{1,0:T(8,128)(2,1)S(1)}, bf16[1024,128]{1,0:T(8,128)(2,1)}, u32[]{:S(2)}, u32[]{:S(2)}) collective-permute-start(bf16[1024,128]{1,0:T(8,128)(2,1)S(1)} %get-tuple-element.127), channel_id=1, source_target_pairs={{0,16},{4,20},{8,24},{12,28},{16,0},{20,4},{24,8},{28,12},{1,17},{... | collective-permute-start | bytes 786440 | tf_op jit(solution)/shard_map/ppermute | solution.py:443
  173.2 1.4 collective-permute-start.15
  175.2 14.4 %collective-permute-done.24 = bf16[1024,128]{1,0:T(8,128)(2,1)S(1)} collective-permute-done((bf16[1024,128]{1,0:T(8,128)(2,1)S(1)}, bf16[1024,128]{1,0:T(8,128)(2,1)S(1)}, u32[]{:S(2)}, u32[]{:S(2)}) %collective-permute-start.24) | collective-permute-done | bytes 262176 | tf_op jit(solution)/shard_map/ppermute | solution.py:443
  189.7 1.4 collective-permute-start.17
  191.1 3.0 %unpack.4 = (bf16[1,24,256,128]{3,2,1,0:T(8,128)(2,1)}, bf16[1,24,256,128]{3,2,1,0:T(8,128)(2,1)}, bf16[1,24,256,128]{3,2,1,0:T(8,128)(2,1)}, bf16[1,24,256,128]{3,2,1,0:T(8,128)(2,1)}, f32[8,128]{1,0:T(8,128)}) custom-call(s32[4]{0:T(128)} %pad_add_fusion.info, bf16[1,24,256,128]{3,2,1,0:T(8,128)(2,1)} %bitcast.31, bf16[1,24,256,128]{3,2,1,0:T(8,128)(2,1)} %bitcast.39, ...), custom_call_target="tpu_custom_call" | custom-call | flops 2000000 | bytes 1179648 | tf_op jit(solution)/shard_map/unpack/pallas_call | solution.py:294
  194.1 4.9 %unpack.5 = (bf16[1,24,256,128]{3,2,1,0:T(8,128)(2,1)}, bf16[1,24,256,128]{3,2,1,0:T(8,128)(2,1)}, bf16[1,24,256,128]{3,2,1,0:T(8,128)(2,1)}, bf16[1,24,256,128]{3,2,1,0:T(8,128)(2,1)}, f32[8,128]{1,0:T(8,128)}) custom-call(s32[4]{0:T(128)} %pad_add_fusion.info, ...), custom_call_target="tpu_custom_call", output_to_operand_aliasing={{0}: (7, {}), {1}: (8, {}), {2}: (9, {}), {3}: (10, {})} | custom-call | flops 6000000 | bytes 3538944 | tf_op jit(solution)/shard_map/unpack/pallas_call | solution.py:294
  199.0 5.4 %unpack.6 = (bf16[1,24,256,128]{3,2,1,0:T(8,128)(2,1)}, bf16[1,24,256,128]{3,2,1,0:T(8,128)(2,1)}, bf16[1,24,256,128]{3,2,1,0:T(8,128)(2,1)}, bf16[1,24,256,128]{3,2,1,0:T(8,128)(2,1)}, f32[8,128]{1,0:T(8,128)}) custom-call(s32[4]{0:T(128)} %pad_add_fusion.info, ...), custom_call_target="tpu_custom_call", output_to_operand_aliasing={{0}: (7, {}), {1}: (8, {}), {2}: (9, {}), {3}: (10, {})} | custom-call | flops 8000000 | bytes 4718592 | tf_op jit(solution)/shard_map/unpack/pallas_call | solution.py:294
  204.4 1.2 slice.47
  205.6 1.9 fusion.3
  208.4 5.3 %all-to-all-start = ((bf16[4,256,128]{1,2,0:T(8,128)(2,1)}), bf16[4,256,128]{1,2,0:T(8,128)(2,1)S(1)}, u32[]{:S(2)}, u32[]{:S(2)}) async-start(bf16[4,256,128]{1,2,0:T(8,128)(2,1)} %copy.39), calls=%async_computation | async-start | bytes 524288 | tf_op jit(solution)/shard_map/all_to_all | solution.py:446
  214.7 5.4 %unpack.7 = (bf16[1,24,256,128]{3,2,1,0:T(8,128)(2,1)}, bf16[1,24,256,128]{3,2,1,0:T(8,128)(2,1)}, bf16[1,24,256,128]{3,2,1,0:T(8,128)(2,1)}, bf16[1,24,256,128]{3,2,1,0:T(8,128)(2,1)}, f32[8,128]{1,0:T(8,128)}) custom-call(s32[4]{0:T(128)} %pad_add_fusion.info, ...), custom_call_target="tpu_custom_call", output_to_operand_aliasing={{0}: (7, {}), {1}: (8, {}), {2}: (9, {}), {3}: (10, {})} | custom-call | flops 8000000 | bytes 4718592 | tf_op jit(solution)/shard_map/unpack/pallas_call | solution.py:294
  (84 shorter events, 17.9 us)
Async XLA Ops:
  6.0 18.5 %collective-permute-start = (bf16[768,256]{1,0:T(8,128)(2,1)}, bf16[768,256]{1,0:T(8,128)(2,1)S(1)}, u32[]{:S(2)}, u32[]{:S(2)}) collective-permute-start(bf16[768,256]{1,0:T(8,128)(2,1)} %get-tuple-element.66), channel_id=1, source_target_pairs={{0,1},{1,0},{2,3},{3,2},{4,5},{5,4},{6,7},{7,6},{8,9},{9,8},{10,11... | collective-permute-start | bytes 1179656 | tf_op jit(solution)/shard_map/ppermute | solution.py:277
  6.5 18.4 %collective-permute-start.1 = (bf16[768,256]{1,0:T(8,128)(2,1)}, bf16[768,256]{1,0:T(8,128)(2,1)S(1)}, u32[]{:S(2)}, u32[]{:S(2)}) collective-permute-start(bf16[768,256]{1,0:T(8,128)(2,1)} %get-tuple-element.67), channel_id=1, source_target_pairs={{0,2},{1,3},{2,0},{3,1},{4,6},{5,7},{6,4},{7,5},{8,10},{9,11},{10,... | collective-permute-start | bytes 1179656 | tf_op jit(solution)/shard_map/ppermute | solution.py:277
  8.1 18.4 %collective-permute-start.2 = (bf16[768,256]{1,0:T(8,128)(2,1)}, bf16[768,256]{1,0:T(8,128)(2,1)S(1)}, u32[]{:S(2)}, u32[]{:S(2)}) collective-permute-start(bf16[768,256]{1,0:T(8,128)(2,1)} %get-tuple-element.68), channel_id=1, source_target_pairs={{0,3},{1,2},{2,1},{3,0},{4,7},{5,6},{6,5},{7,4},{8,11},{9,10},{10,... | collective-permute-start | bytes 1179656 | tf_op jit(solution)/shard_map/ppermute | solution.py:277
  24.5 1.9 copy-start
  24.9 1.5 copy-start.1
  28.2 5.2 %collective-permute-start.3 = (bf16[512,256]{1,0:T(8,128)(2,1)S(1)}, bf16[512,256]{1,0:T(8,128)(2,1)S(1)}, u32[]{:S(2)}, u32[]{:S(2)}) collective-permute-start(bf16[512,256]{1,0:T(8,128)(2,1)S(1)} %slice.36), channel_id=1, source_target_pairs={{0,4},{4,0},{8,12},{12,8},{16,20},{20,16},{24,28},{28,24},{1,5},{5... | collective-permute-start | bytes 786440 | tf_op jit(solution)/shard_map/ppermute | solution.py:280
  29.2 5.2 %collective-permute-start.4 = (bf16[512,256]{1,0:T(8,128)(2,1)S(1)}, bf16[512,256]{1,0:T(8,128)(2,1)S(1)}, u32[]{:S(2)}, u32[]{:S(2)}) collective-permute-start(bf16[512,256]{1,0:T(8,128)(2,1)S(1)} %slice.37), channel_id=1, source_target_pairs={{0,4},{4,0},{8,12},{12,8},{16,20},{20,16},{24,28},{28,24},{1,5},{5... | collective-permute-start | bytes 786440 | tf_op jit(solution)/shard_map/ppermute | solution.py:280
  30.7 3.7 %collective-permute-start.5 = (bf16[512,256]{1,0:T(8,128)(2,1)S(1)}, bf16[512,256]{1,0:T(8,128)(2,1)S(1)}, u32[]{:S(2)}, u32[]{:S(2)}) collective-permute-start(bf16[512,256]{1,0:T(8,128)(2,1)S(1)} %slice.38), channel_id=1, source_target_pairs={{0,4},{4,0},{8,12},{12,8},{16,20},{20,16},{24,28},{28,24},{1,5},{5... | collective-permute-start | bytes 786440 | tf_op jit(solution)/shard_map/ppermute | solution.py:280
  30.8 18.8 %collective-permute-start.6 = (bf16[768,256]{1,0:T(8,128)(2,1)}, bf16[768,256]{1,0:T(8,128)(2,1)S(1)}, u32[]{:S(2)}, u32[]{:S(2)}) collective-permute-start(bf16[768,256]{1,0:T(8,128)(2,1)} %get-tuple-element.78), channel_id=1, source_target_pairs={{0,1},{1,0},{2,3},{3,2},{4,5},{5,4},{6,7},{7,6},{8,9},{9,8},{10,11... | collective-permute-start | bytes 1179656 | tf_op jit(solution)/shard_map/ppermute | solution.py:277
  31.8 19.7 %collective-permute-start.7 = (bf16[768,256]{1,0:T(8,128)(2,1)}, bf16[768,256]{1,0:T(8,128)(2,1)S(1)}, u32[]{:S(2)}, u32[]{:S(2)}) collective-permute-start(bf16[768,256]{1,0:T(8,128)(2,1)} %get-tuple-element.79), channel_id=1, source_target_pairs={{0,2},{1,3},{2,0},{3,1},{4,6},{5,7},{6,4},{7,5},{8,10},{9,11},{10,... | collective-permute-start | bytes 1179656 | tf_op jit(solution)/shard_map/ppermute | solution.py:277
  33.4 18.5 %collective-permute-start.8 = (bf16[768,256]{1,0:T(8,128)(2,1)}, bf16[768,256]{1,0:T(8,128)(2,1)S(1)}, u32[]{:S(2)}, u32[]{:S(2)}) collective-permute-start(bf16[768,256]{1,0:T(8,128)(2,1)} %get-tuple-element.80), channel_id=1, source_target_pairs={{0,3},{1,2},{2,1},{3,0},{4,7},{5,6},{6,5},{7,4},{8,11},{9,10},{10,... | collective-permute-start | bytes 1179656 | tf_op jit(solution)/shard_map/ppermute | solution.py:277
  47.2 36.9 %collective-permute-start.12 = (bf16[1280,256]{1,0:T(8,128)(2,1)}, bf16[1280,256]{1,0:T(8,128)(2,1)S(1)}, u32[]{:S(2)}, u32[]{:S(2)}) collective-permute-start(bf16[1280,256]{1,0:T(8,128)(2,1)} %get-tuple-element.93), channel_id=1, source_target_pairs={{0,1},{1,0},{2,3},{3,2},{4,5},{5,4},{6,7},{7,6},{8,9},{9,8},{10,11... | collective-permute-start | bytes 1966088 | tf_op jit(solution)/shard_map/ppermute | solution.py:277
  48.1 37.4 %collective-permute-start.13 = (bf16[1280,256]{1,0:T(8,128)(2,1)}, bf16[1280,256]{1,0:T(8,128)(2,1)S(1)}, u32[]{:S(2)}, u32[]{:S(2)}) collective-permute-start(bf16[1280,256]{1,0:T(8,128)(2,1)} %get-tuple-element.94), channel_id=1, source_target_pairs={{0,2},{1,3},{2,0},{3,1},{4,6},{5,7},{6,4},{7,5},{8,10},{9,11},{10,... | collective-permute-start | bytes 1966088 | tf_op jit(solution)/shard_map/ppermute | solution.py:277
  49.6 2.3 %copy-start.14 = (bf16[768,256]{1,0:T(8,128)(2,1)}, bf16[768,256]{1,0:T(8,128)(2,1)S(1)}, u32[]{:S(2)}) copy-start(bf16[768,256]{1,0:T(8,128)(2,1)S(1)} %collective-permute-done.6.refs_8_) | copy-start | bytes 1179652
  49.6 35.9 %collective-permute-start.14 = (bf16[1280,256]{1,0:T(8,128)(2,1)}, bf16[1280,256]{1,0:T(8,128)(2,1)S(1)}, u32[]{:S(2)}, u32[]{:S(2)}) collective-permute-start(bf16[1280,256]{1,0:T(8,128)(2,1)} %get-tuple-element.95), channel_id=1, source_target_pairs={{0,3},{1,2},{2,1},{3,0},{4,7},{5,6},{6,5},{7,4},{8,11},{9,10},{10,... | collective-permute-start | bytes 1966088 | tf_op jit(solution)/shard_map/ppermute | solution.py:277
  82.0 43.7 %collective-permute-start.9 = (bf16[1792,256]{1,0:T(8,128)(2,1)}, bf16[1792,256]{1,0:T(8,128)(2,1)S(1)}, u32[]{:S(2)}, u32[]{:S(2)}) collective-permute-start(bf16[1792,256]{1,0:T(8,128)(2,1)} %get-tuple-element.89), channel_id=1, source_target_pairs={{0,1},{1,0},{2,3},{3,2},{4,5},{5,4},{6,7},{7,6},{8,9},{9,8},{10,11... | collective-permute-start | bytes 2752520 | tf_op jit(solution)/shard_map/ppermute | solution.py:277
  83.5 43.7 %collective-permute-start.10 = (bf16[1792,256]{1,0:T(8,128)(2,1)}, bf16[1792,256]{1,0:T(8,128)(2,1)S(1)}, u32[]{:S(2)}, u32[]{:S(2)}) collective-permute-start(bf16[1792,256]{1,0:T(8,128)(2,1)} %get-tuple-element.90), channel_id=1, source_target_pairs={{0,2},{1,3},{2,0},{3,1},{4,6},{5,7},{6,4},{7,5},{8,10},{9,11},{10,... | collective-permute-start | bytes 2752520 | tf_op jit(solution)/shard_map/ppermute | solution.py:277
  84.1 1.5 copy-start.9
  84.1 43.1 %collective-permute-start.11 = (bf16[1792,256]{1,0:T(8,128)(2,1)}, bf16[1792,256]{1,0:T(8,128)(2,1)}, u32[]{:S(2)}, u32[]{:S(2)}) collective-permute-start(bf16[1792,256]{1,0:T(8,128)(2,1)} %get-tuple-element.91), channel_id=1, source_target_pairs={{0,3},{1,2},{2,1},{3,0},{4,7},{5,6},{6,5},{7,4},{8,11},{9,10},{10,... | collective-permute-start | bytes 2752520 | tf_op jit(solution)/shard_map/ppermute | solution.py:277
  123.6 41.3 %collective-permute-start.18 = (bf16[1024,256]{1,0:T(8,128)(2,1)}, bf16[1024,256]{1,0:T(8,128)(2,1)S(1)}, u32[]{:S(2)}, u32[]{:S(2)}) collective-permute-start(bf16[1024,256]{1,0:T(8,128)(2,1)} %get-tuple-element.103), channel_id=1, source_target_pairs={{0,1},{1,0},{2,3},{3,2},{4,5},{5,4},{6,7},{7,6},{8,9},{9,8},{10,11... | collective-permute-start | bytes 1572872 | tf_op jit(solution)/shard_map/ppermute | solution.py:277
  125.1 39.9 %collective-permute-start.19 = (bf16[1024,256]{1,0:T(8,128)(2,1)}, bf16[1024,256]{1,0:T(8,128)(2,1)S(1)}, u32[]{:S(2)}, u32[]{:S(2)}) collective-permute-start(bf16[1024,256]{1,0:T(8,128)(2,1)} %get-tuple-element.104), channel_id=1, source_target_pairs={{0,2},{1,3},{2,0},{3,1},{4,6},{5,7},{6,4},{7,5},{8,10},{9,11},{10,... | collective-permute-start | bytes 1572872 | tf_op jit(solution)/shard_map/ppermute | solution.py:277
  125.7 1.5 copy-start.7
  125.7 39.3 %collective-permute-start.20 = (bf16[1024,256]{1,0:T(8,128)(2,1)}, bf16[1024,256]{1,0:T(8,128)(2,1)S(1)}, u32[]{:S(2)}, u32[]{:S(2)}) collective-permute-start(bf16[1024,256]{1,0:T(8,128)(2,1)} %get-tuple-element.105), channel_id=1, source_target_pairs={{0,3},{1,2},{2,1},{3,0},{4,7},{5,6},{6,5},{7,4},{8,11},{9,10},{10,... | collective-permute-start | bytes 1572872 | tf_op jit(solution)/shard_map/ppermute | solution.py:277
  166.1 2.9 %copy-start.6 = (bf16[4,1024,128]{2,1,0:T(8,128)(2,1)S(1)}, bf16[4,1024,128]{2,1,0:T(8,128)(2,1)}, u32[]{:S(2)}) copy-start(bf16[4,1024,128]{2,1,0:T(8,128)(2,1)} %get-tuple-element.122) | copy-start | bytes 3145732
  166.1 2.9 %collective-permute-start.21 = (bf16[4,1024,128]{2,1,0:T(8,128)(2,1)}, bf16[4,1024,128]{2,1,0:T(8,128)(2,1)S(1)}, u32[]{:S(2)}, u32[]{:S(2)}) collective-permute-start(bf16[4,1024,128]{2,1,0:T(8,128)(2,1)} %hold.5), channel_id=1, source_target_pairs={{0,4},{4,0},{8,12},{12,8},{16,20},{20,16},{24,28},{28,24},{1,5},{5... | collective-permute-start | bytes 3145736 | tf_op jit(solution)/shard_map/ppermute | solution.py:280
  169.2 20.4 %collective-permute-start.24 = (bf16[1024,128]{1,0:T(8,128)(2,1)S(1)}, bf16[1024,128]{1,0:T(8,128)(2,1)S(1)}, u32[]{:S(2)}, u32[]{:S(2)}) collective-permute-start(bf16[1024,128]{1,0:T(8,128)(2,1)S(1)} %get-tuple-element.126), channel_id=1, source_target_pairs={{0,24},{4,28},{8,16},{12,20},{16,8},{20,12},{24,0},{28,4},{1,25},{... | collective-permute-start | bytes 786440 | tf_op jit(solution)/shard_map/ppermute | solution.py:443
  169.7 35.9 %collective-permute-start.23 = (bf16[1024,128]{1,0:T(8,128)(2,1)S(1)}, bf16[1024,128]{1,0:T(8,128)(2,1)}, u32[]{:S(2)}, u32[]{:S(2)}) collective-permute-start(bf16[1024,128]{1,0:T(8,128)(2,1)S(1)} %get-tuple-element.127), channel_id=1, source_target_pairs={{0,16},{4,20},{8,24},{12,28},{16,0},{20,4},{24,8},{28,12},{1,17},{... | collective-permute-start | bytes 786440 | tf_op jit(solution)/shard_map/ppermute | solution.py:443
  173.2 32.4 %collective-permute-start.22 = (bf16[1024,128]{1,0:T(8,128)(2,1)S(1)}, bf16[1024,128]{1,0:T(8,128)(2,1)}, u32[]{:S(2)}, u32[]{:S(2)}) collective-permute-start(bf16[1024,128]{1,0:T(8,128)(2,1)S(1)} %get-tuple-element.125), channel_id=1, source_target_pairs={{0,8},{4,12},{8,0},{12,4},{16,24},{20,28},{24,16},{28,20},{1,9},{5... | collective-permute-start | bytes 786440 | tf_op jit(solution)/shard_map/ppermute | solution.py:443
  173.2 40.5 %collective-permute-start.15 = (bf16[1024,256]{1,0:T(8,128)(2,1)}, bf16[1024,256]{1,0:T(8,128)(2,1)S(1)}, u32[]{:S(2)}, u32[]{:S(2)}) collective-permute-start(bf16[1024,256]{1,0:T(8,128)(2,1)} %get-tuple-element.99), channel_id=1, source_target_pairs={{0,1},{1,0},{2,3},{3,2},{4,5},{5,4},{6,7},{7,6},{8,9},{9,8},{10,11... | collective-permute-start | bytes 1572872 | tf_op jit(solution)/shard_map/ppermute | solution.py:277
  174.6 39.1 %collective-permute-start.16 = (bf16[1024,256]{1,0:T(8,128)(2,1)}, bf16[1024,256]{1,0:T(8,128)(2,1)S(1)}, u32[]{:S(2)}, u32[]{:S(2)}) collective-permute-start(bf16[1024,256]{1,0:T(8,128)(2,1)} %get-tuple-element.100), channel_id=1, source_target_pairs={{0,2},{1,3},{2,0},{3,1},{4,6},{5,7},{6,4},{7,5},{8,10},{9,11},{10,... | collective-permute-start | bytes 1572872 | tf_op jit(solution)/shard_map/ppermute | solution.py:277
  189.7 24.1 %collective-permute-start.17 = (bf16[1024,256]{1,0:T(8,128)(2,1)}, bf16[1024,256]{1,0:T(8,128)(2,1)}, u32[]{:S(2)}, u32[]{:S(2)}) collective-permute-start(bf16[1024,256]{1,0:T(8,128)(2,1)} %get-tuple-element.101), channel_id=1, source_target_pairs={{0,3},{1,2},{2,1},{3,0},{4,7},{5,6},{6,5},{7,4},{8,11},{9,10},{10,... | collective-permute-start | bytes 1572872 | tf_op jit(solution)/shard_map/ppermute | solution.py:277
  208.4 11.8 %all-to-all-start = ((bf16[4,256,128]{1,2,0:T(8,128)(2,1)}), bf16[4,256,128]{1,2,0:T(8,128)(2,1)S(1)}, u32[]{:S(2)}, u32[]{:S(2)}) async-start(bf16[4,256,128]{1,2,0:T(8,128)(2,1)} %copy.39), calls=%async_computation | async-start | bytes 524288 | tf_op jit(solution)/shard_map/all_to_all | solution.py:446
  (14 other events, 12.3 us)
